TPU v7x, 32 devices: a whole 2x2x4 slice. The times are simulated.
32 devices in a mesh: dp: 8 (over z, x), tensor: 4 (over y, core).
Axes of the slice: x: 2, y: 2, z: 4, core: 2. Of those that a mesh axis runs over, the one named last changes fastest.
Arguments:
- hidden_in: bfloat16 [16384, 640], P('dp'), may hold values from -6 to 6
- query_weight: bfloat16 [640, 1024], P(None, 'tensor'), may hold values from -0.25 to 0.25
- key_weight: bfloat16 [640, 256], replicated, may hold values from -0.25 to 0.25
- value_weight: bfloat16 [640, 256], replicated, may hold values from -0.25 to 0.25
- output_weight: bfloat16 [1024, 640], P('tensor'), may hold values from -0.1875 to 0.1875
- gate_weight: bfloat16 [640, 2048], P(None, 'tensor'), may hold values from -0.25 to 0.25
- up_weight: bfloat16 [640, 2048], P(None, 'tensor'), may hold values from -0.25 to 0.25
- down_weight: bfloat16 [2048, 640], P('tensor'), may hold values from -0.125 to 0.125
- pre_attention: float32 [640], replicated, may hold values from -0.5 to 0.5
- query_norm: float32 [256], replicated, may hold values from -0.5 to 0.5
- key_norm: float32 [256], replicated, may hold values from -0.5 to 0.5
- post_attention: float32 [640], replicated, may hold values from -0.5 to 0.5
- pre_feedforward: float32 [640], replicated, may hold values from -0.5 to 0.5
- post_feedforward: float32 [640], replicated, may hold values from -0.5 to 0.5
- segments: int32 [16384], P('dp'), may hold values from 0 to 15, as said below
- positions: int32 [16384], P('dp'), may hold values from 0 to 511, as said below
- cotangent: bfloat16 [16384, 640], P('dp'), may hold values from -6 to 6
Outputs:
- hidden_out: bfloat16 [16384, 640], P('dp')
- grad_input: float32 [16384, 640], P('dp')
- grad_query_weight: float32 [640, 1024], P(None, 'tensor')
- grad_key_weight: float32 [640, 256], replicated
- grad_value_weight: float32 [640, 256], replicated
- grad_output_weight: float32 [1024, 640], P('tensor')
- grad_gate_weight: float32 [640, 2048], P(None, 'tensor')
- grad_up_weight: float32 [640, 2048], P(None, 'tensor')
- grad_down_weight: float32 [2048, 640], P('tensor')
- grad_pre_attention: float32 [640], replicated
- grad_query_norm: float32 [256], replicated
- grad_key_norm: float32 [256], replicated
- grad_post_attention: float32 [640], replicated
- grad_pre_feedforward: float32 [640], replicated
- grad_post_feedforward: float32 [640], replicated
Inputs may be any that keep to these rules, and one draw needn't show every extreme that they name: `segments`: within each aligned block of 512 tokens the document numbers start at 0 at the block's first token and rise by 0 or 1 from one token to the next. `positions`: each token's position is its distance from the first token of its document in the same block.
All inputs are finite; a program needn't handle non-finite values.
Results may differ from a plain program's by a relative error of at most 0.02.
Values may be sent and summed in bfloat16 or wider, within the bound.
A program may use at most 128 MiB of HBM per device.

v0:
```python
import jax
import jax.numpy as jnp
from jax import lax
from jax.sharding import PartitionSpec as P

LEN = 512
epsilon = 1e-06
rope_base = 1000000.0
masked_score = -1e30


def normed(values, norm_gain):
    inverse = lax.rsqrt(jnp.mean(values * values, axis=-1, keepdims=True) + epsilon)
    return values * inverse * (1.0 + norm_gain)


def rotary(values, cosine, sine_table):
    half_width = values.shape[-1] // 2
    front_half = values[..., :half_width]
    second = values[..., half_width:]
    return jnp.concatenate(
        [front_half * cosine - second * sine_table, second * cosine + front_half * sine_table],
        axis=-1,
    )


def rotary_tables(positions, head_width):
    steps_half = jnp.arange(head_width // 2).astype(jnp.float32)
    frequency = jnp.power(jnp.float32(rope_base), -2.0 * steps_half / head_width)
    angles = positions.astype(jnp.float32)[:, None] * frequency[None, :]
    return (jnp.cos(angles), jnp.sin(angles))


def gated(gate_proj, up_proj):
    return jax.nn.gelu(gate_proj, approximate=True) * up_proj


def pack_mask(segment):
    offsets = jnp.arange(segment.shape[0])
    return (segment[:, None] == segment[None, :]) & (offsets[None, :] <= offsets[:, None])


def pack_scores(queries, key_rows, segment):
    score_scale = queries.shape[-1] ** (-0.5)
    scores = (
        jnp.einsum("ihd,jd->hij", queries, key_rows, preferred_element_type=jnp.float32)
        * score_scale
    )
    return jnp.where(pack_mask(segment)[None], scores, masked_score)


def attend_pack(inputs):
    queries, key_rows, values, segment = inputs
    scores = pack_scores(queries, key_rows, segment)
    top_score = jnp.max(scores, axis=-1, keepdims=True)
    log_total = top_score + jnp.log(jnp.sum(jnp.exp(scores - top_score), axis=-1, keepdims=True))
    prob_low = jnp.exp(scores - log_total).astype(jnp.bfloat16)
    mixture = jnp.einsum("hij,jd->ihd", prob_low, values, preferred_element_type=jnp.float32)
    return (mixture.astype(jnp.bfloat16), log_total)


def attend_back(inputs):
    queries, key_rows, values, segment, log_total, mixture_grad = inputs
    score_scale = queries.shape[-1] ** (-0.5)
    probability = jnp.exp(pack_scores(queries, key_rows, segment) - log_total)
    prob_low = probability.astype(jnp.bfloat16)
    value_grad = jnp.einsum(
        "hij,ihd->jhd", prob_low, mixture_grad, preferred_element_type=jnp.float32
    )
    prob_grad = jnp.einsum("ihd,jd->hij", mixture_grad, values, preferred_element_type=jnp.float32)
    row_terms = jnp.sum(probability * prob_grad, axis=-1, keepdims=True)
    score_grad = (probability * (prob_grad - row_terms)).astype(jnp.bfloat16)
    query_grad = (
        jnp.einsum("hij,jd->ihd", score_grad, key_rows, preferred_element_type=jnp.float32)
        * score_scale
    )
    key_grad = (
        jnp.einsum("hij,ihd->jhd", score_grad, queries, preferred_element_type=jnp.float32)
        * score_scale
    )
    return (query_grad, key_grad, value_grad.astype(jnp.bfloat16))


def run_layer(
    hidden_in,
    query_weight,
    key_weight,
    value_weight,
    output_weight,
    gate_weight,
    up_weight,
    down_weight,
    pre_attention,
    query_norm,
    key_norm,
    post_attention,
    pre_feedforward,
    post_feedforward,
    segments,
    positions,
    cotangent,
    reducers,
    feed_hook,
):
    attention_reduce, feed_reduce, feed_back_reduce, attention_back_reduce = reducers
    tokens = hidden_in.shape[0]
    pack_length = LEN
    pack_count = tokens // pack_length
    head_width = key_weight.shape[1]
    local_heads = query_weight.shape[1] // head_width
    hidden = hidden_in.astype(jnp.float32)
    cosine, sine_table = rotary_tables(positions, head_width)

    def head_path(projected, norm_gain):
        return rotary(normed(projected, norm_gain), cosine[:, None, :], sine_table[:, None, :])

    normed_value, pre_back = jax.vjp(normed, hidden, pre_attention)
    normed_in = normed_value.astype(jnp.bfloat16)
    query_proj = jnp.dot(normed_in, query_weight, preferred_element_type=jnp.float32)
    query_proj = query_proj.reshape(tokens, local_heads, head_width)
    key_proj = jnp.dot(normed_in, key_weight, preferred_element_type=jnp.float32)
    value_low = jnp.dot(normed_in, value_weight, preferred_element_type=jnp.float32).astype(
        jnp.bfloat16
    )
    query_rot, query_back = jax.vjp(head_path, query_proj, query_norm)
    key_heads = key_proj[:, None, :]
    key_rot, key_back = jax.vjp(head_path, key_heads, key_norm)
    query_packs = query_rot.astype(jnp.bfloat16).reshape(
        pack_count, pack_length, local_heads, head_width
    )
    key_packs = key_rot[:, 0, :].astype(jnp.bfloat16).reshape(pack_count, pack_length, head_width)
    value_packs = value_low.reshape(pack_count, pack_length, head_width)
    segment_packs = segments.reshape(pack_count, pack_length)
    mixture, log_total = lax.map(attend_pack, (query_packs, key_packs, value_packs, segment_packs))
    mixture_low = mixture.reshape(tokens, local_heads * head_width)
    attention = attention_reduce(
        jnp.dot(mixture_low, output_weight, preferred_element_type=jnp.float32)
    )
    post_value, post_att_back = jax.vjp(normed, attention, post_attention)
    middle = hidden + post_value
    mid_value, mid_back = jax.vjp(normed, middle, pre_feedforward)
    normed_mid = mid_value.astype(jnp.bfloat16)
    gate_proj = jnp.dot(normed_mid, gate_weight, preferred_element_type=jnp.float32)
    up_proj = jnp.dot(normed_mid, up_weight, preferred_element_type=jnp.float32)
    product, gated_back = jax.vjp(gated, gate_proj, up_proj)
    product_low = product.astype(jnp.bfloat16)
    feed = feed_reduce(jnp.dot(product_low, down_weight, preferred_element_type=jnp.float32))
    feed_value, feed_out_back = jax.vjp(normed, feed, post_feedforward)
    hidden_out = (middle + feed_value).astype(jnp.bfloat16)
    cotangent_full = cotangent.astype(jnp.float32)
    feed_grad, grad_post_feedforward = feed_out_back(cotangent_full)
    feed_grad_low = feed_grad.astype(jnp.bfloat16)
    grad_down_weight = jnp.einsum(
        "tf,td->fd", product_low, feed_grad_low, preferred_element_type=jnp.float32
    )
    product_grad = jnp.einsum(
        "td,fd->tf", feed_grad_low, down_weight, preferred_element_type=jnp.float32
    )
    gate_grad, up_grad = gated_back(product_grad)
    gate_grad_low = gate_grad.astype(jnp.bfloat16)
    up_grad_low = up_grad.astype(jnp.bfloat16)
    grad_gate_weight = jnp.einsum(
        "td,tf->df", normed_mid, gate_grad_low, preferred_element_type=jnp.float32
    )
    grad_up_weight = jnp.einsum(
        "td,tf->df", normed_mid, up_grad_low, preferred_element_type=jnp.float32
    )
    grad_gate_weight, grad_up_weight, grad_down_weight, grad_post_feedforward = feed_hook(
        (grad_gate_weight, grad_up_weight, grad_down_weight, grad_post_feedforward)
    )
    mid_part = jnp.einsum(
        "tf,df->td", gate_grad_low, gate_weight, preferred_element_type=jnp.float32
    )
    mid_part = mid_part + jnp.einsum(
        "tf,df->td", up_grad_low, up_weight, preferred_element_type=jnp.float32
    )
    mid_normed_grad = feed_back_reduce(mid_part)
    middle_part, grad_pre_feedforward = mid_back(mid_normed_grad)
    middle_grad = cotangent_full + middle_part
    attention_grad, grad_post_attention = post_att_back(middle_grad)
    attention_grad_low = attention_grad.astype(jnp.bfloat16)
    grad_output_weight = jnp.einsum(
        "tk,td->kd", mixture_low, attention_grad_low, preferred_element_type=jnp.float32
    )
    mixture_grad = jnp.einsum(
        "td,kd->tk", attention_grad_low, output_weight, preferred_element_type=jnp.float32
    )
    mixture_grad_packs = mixture_grad.astype(jnp.bfloat16).reshape(
        pack_count, pack_length, local_heads, head_width
    )
    query_rot_grad, key_rot_grad, value_grad_low = lax.map(
        attend_back,
        (query_packs, key_packs, value_packs, segment_packs, log_total, mixture_grad_packs),
    )
    query_grad, grad_query_norm = query_back(
        query_rot_grad.reshape(tokens, local_heads, head_width)
    )
    key_grad, grad_key_norm = key_back(key_rot_grad.reshape(tokens, local_heads, head_width))
    query_grad_low = query_grad.astype(jnp.bfloat16).reshape(tokens, local_heads * head_width)
    key_grad_low = key_grad.astype(jnp.bfloat16)
    value_grad_low = value_grad_low.reshape(tokens, local_heads, head_width)
    grad_query_weight = jnp.einsum(
        "td,tk->dk", normed_in, query_grad_low, preferred_element_type=jnp.float32
    )
    grad_key_weight = jnp.einsum(
        "td,thk->dk", normed_in, key_grad_low, preferred_element_type=jnp.float32
    )
    grad_value_weight = jnp.einsum(
        "td,thk->dk", normed_in, value_grad_low, preferred_element_type=jnp.float32
    )
    in_part = jnp.einsum(
        "tk,dk->td", query_grad_low, query_weight, preferred_element_type=jnp.float32
    )
    in_part = in_part + jnp.einsum(
        "thk,dk->td", key_grad_low, key_weight, preferred_element_type=jnp.float32
    )
    in_part = in_part + jnp.einsum(
        "thk,dk->td", value_grad_low, value_weight, preferred_element_type=jnp.float32
    )
    in_normed_grad = attention_back_reduce(in_part)
    input_part, grad_pre_attention = pre_back(in_normed_grad)
    grad_input = middle_grad + input_part
    return (
        hidden_out,
        grad_input,
        grad_query_weight,
        grad_key_weight,
        grad_value_weight,
        grad_output_weight,
        grad_gate_weight,
        grad_up_weight,
        grad_down_weight,
        grad_pre_attention,
        grad_query_norm,
        grad_key_norm,
        grad_post_attention,
        grad_pre_feedforward,
        grad_post_feedforward,
    )


def on_device(
    hidden_in,
    query_weight,
    key_weight,
    value_weight,
    output_weight,
    gate_weight,
    up_weight,
    down_weight,
    pre_attention,
    query_norm,
    key_norm,
    post_attention,
    pre_feedforward,
    post_feedforward,
    segments,
    positions,
    cotangent,
):

    def attention_reduce(values):
        return lax.psum(values, "tensor")

    def feed_reduce(values):
        return lax.psum(values.astype(jnp.bfloat16), "tensor").astype(jnp.float32)

    def feed_back_reduce(values):
        return lax.psum(values.astype(jnp.bfloat16), "tensor").astype(jnp.float32)

    def attention_back_reduce(values):
        return lax.psum(values.astype(jnp.bfloat16), "tensor").astype(jnp.float32)

    def feed_hook(grads):
        return grads

    (
        hidden_out,
        grad_input,
        grad_query_weight,
        grad_key_weight,
        grad_value_weight,
        grad_output_weight,
        grad_gate_weight,
        grad_up_weight,
        grad_down_weight,
        grad_pre_attention,
        grad_query_norm,
        grad_key_norm,
        grad_post_attention,
        grad_pre_feedforward,
        grad_post_feedforward,
    ) = run_layer(
        hidden_in,
        query_weight,
        key_weight,
        value_weight,
        output_weight,
        gate_weight,
        up_weight,
        down_weight,
        pre_attention,
        query_norm,
        key_norm,
        post_attention,
        pre_feedforward,
        post_feedforward,
        segments,
        positions,
        cotangent,
        (attention_reduce, feed_reduce, feed_back_reduce, attention_back_reduce),
        feed_hook,
    )
    grad_key_weight, grad_value_weight, grad_query_norm, grad_key_norm = lax.psum(
        (grad_key_weight, grad_value_weight, grad_query_norm, grad_key_norm), ("dp", "tensor")
    )
    (
        grad_query_weight,
        grad_output_weight,
        grad_gate_weight,
        grad_up_weight,
        grad_down_weight,
        grad_pre_attention,
        grad_post_attention,
        grad_pre_feedforward,
        grad_post_feedforward,
    ) = lax.psum(
        (
            grad_query_weight,
            grad_output_weight,
            grad_gate_weight,
            grad_up_weight,
            grad_down_weight,
            grad_pre_attention,
            grad_post_attention,
            grad_pre_feedforward,
            grad_post_feedforward,
        ),
        "dp",
    )
    return (
        hidden_out,
        grad_input,
        grad_query_weight,
        grad_key_weight,
        grad_value_weight,
        grad_output_weight,
        grad_gate_weight,
        grad_up_weight,
        grad_down_weight,
        grad_pre_attention,
        grad_query_norm,
        grad_key_norm,
        grad_post_attention,
        grad_pre_feedforward,
        grad_post_feedforward,
    )


def solution(mesh):
    placed = (
        P("dp", None),
        P(None, "tensor"),
        P(),
        P(),
        P("tensor", None),
        P(None, "tensor"),
        P(None, "tensor"),
        P("tensor", None),
        P(),
        P(),
        P(),
        P(),
        P(),
        P(),
        P("dp"),
        P("dp"),
        P("dp", None),
    )
    return jax.shard_map(
        on_device,
        mesh=mesh,
        in_specs=placed,
        out_specs=(
            P("dp", None),
            P("dp", None),
            P(None, "tensor"),
            P(),
            P(),
            P("tensor", None),
            P(None, "tensor"),
            P(None, "tensor"),
            P("tensor", None),
            P(),
            P(),
            P(),
            P(),
            P(),
            P(),
        ),
        check_vma=False,
    )
```

profile of v0, /device:TPU:0, one launch (start us, length us, event | category | flops | bytes accessed | tf_op | source)
XLA Modules:
  0.0 909.8 jit_solution(12823472843531258651)
XLA Ops:
  7.3 2.5 fusion.63
  10.8 2.4 multiply_reduce_fusion.6
  13.2 2.3 multiply_reduce_fusion.5
  15.6 3.0 copy.42
  18.6 2.6 multiply_bitcast_fusion
  21.3 5.7 fusion.99
  31.1 2.3 pad_maximum_fusion
  33.4 2.3 copy.56
  35.6 3.7 convolution_convert_fusion.4
  40.0 2.3 pad_maximum_fusion.1
  43.3 26.9 %while.26 = (s32[]{:T(128)}, bf16[4,512,1,256]{3,1,0,2:T(8,128)(2,1)}, f32[4,1,512,1]{2,3,1,0:T(1,128)}, bf16[4,512,256]{2,1,0:T(8,128)(2,1)}, s32[4,512]{1,0:T(...) while((s32[]{:T(128)}, bf16[4,512,1,256]{3,1,0,2:T(8,128)(2,1)}, ...), condition=%wide.region_6.7_spmd, body=%wide.region_3.6_spmd.sunk | while | flops 271187456 | bytes 5272153 | solution.py:134
  70.2 4.6 fusion.115
  75.6 104.7 %all-reduce.15.cloned.1.call-done = f32[2048,640]{1,0:T(8,128)} async-done(((f32[2048,640]{1,0:T(8,128)}), f32[2048,640]{1,0:T(8,128)}) %all-reduce.15.cloned.1.call-update) | async-done | bytes 5242896 | tf_op jit(solution)/shard_map/psum | solution.py:263
  180.3 3.0 multiply_reduce_fusion.4
  190.1 4.1 multiply_convert_fusion.3
  195.5 3.3 convolution_convert_fusion.2
  199.4 59.6 %all-reduce.17.cloned.1.call-done = bf16[2048,640]{1,0:T(8,128)(2,1)} async-done(((bf16[2048,640]{1,0:T(8,128)(2,1)}), bf16[2048,640]{1,0:T(8,128)(2,1)}) %all-reduce.17.cloned.1.call-update) | async-done | bytes 2621456 | tf_op jit(solution)/shard_map/psum | solution.py:266
  259.0 2.5 fusion.61
  261.5 4.2 fusion.57
  267.9 4.9 multiply_convert_fusion.2
  274.8 3.3 add_convert_fusion.1
  278.4 5.3 fusion.126
  283.6 54.6 %all-reduce.19.cloned.1.call-done = bf16[2048,640]{1,0:T(8,128)(2,1)} async-done(((bf16[2048,640]{1,0:T(8,128)(2,1)}), bf16[2048,640]{1,0:T(8,128)(2,1)}) %all-reduce.19.cloned.1.call-update) | async-done | bytes 2621456 | tf_op jit(solution)/shard_map/psum | solution.py:269
  338.3 4.4 fusion.55
  343.1 7.7 multiply_reduce_fusion.1
  355.8 125.7 %while.27 = (s32[]{:T(128)}, f32[4,512,1,256]{1,0,3,2:T(4,128)}, f32[4,512,1,256]{1,0,3,2:T(4,128)}, bf16[4,512,1,256]{3,1,0,2:T(8,128)(2,1)}, bf16[4,512,256]{2...) while((s32[]{:T(128)}, f32[4,512,1,256]{1,0,3,2:T(4,128)}, ...), condition=%wide.region_18.19_spmd, body=%wide.region_16.18_spmd.sunk | while | flops 674627072 | bytes 16275081 | solution.py:191
  362.1 11.0 %dynamic_update_slice.30 = f32[4,512,1,256]{1,0,3,2:T(4,128)} dynamic-update-slice(f32[4,512,1,256]{1,0,3,2:T(4,128)} %get-tuple-element.387, f32[1,512,1,256]{1,0,3,2:T(1,128)S(1)} %copy.93, s32[]{:T(128)} %get-tuple-element.385, s32[]{:T(128)} %constant.83.clone.1..sunk, s32[]{:T(128)} %constant.83.clone.1..sunk, s32[]{:T(128)} %constant.83.clone.1..sunk) | dynamic-update-slice | bytes 1048580 | tf_op jit(solution)/shard_map/while/body/jit(dynamic_update_index_in_dim)/dynamic_update_slice | solution.py:191
  374.9 11.1 %dynamic_update_slice.29 = f32[4,512,1,256]{1,0,3,2:T(4,128)} dynamic-update-slice(f32[4,512,1,256]{1,0,3,2:T(4,128)} %get-tuple-element.386, f32[1,512,1,256]{1,0,3,2:T(1,128)S(1)} %copy.92, s32[]{:T(128)} %get-tuple-element.385, s32[]{:T(128)} %constant.83.clone.1..sunk, s32[]{:T(128)} %constant.83.clone.1..sunk, s32[]{:T(128)} %constant.83.clone.1..sunk) | dynamic-update-slice | bytes 1048580 | tf_op jit(solution)/shard_map/while/body/jit(dynamic_update_index_in_dim)/dynamic_update_slice | solution.py:191
  393.5 11.0 %dynamic_update_slice.30 = f32[4,512,1,256]{1,0,3,2:T(4,128)} dynamic-update-slice(f32[4,512,1,256]{1,0,3,2:T(4,128)} %get-tuple-element.387, f32[1,512,1,256]{1,0,3,2:T(1,128)S(1)} %copy.93, s32[]{:T(128)} %get-tuple-element.385, s32[]{:T(128)} %constant.83.clone.1..sunk, s32[]{:T(128)} %constant.83.clone.1..sunk, s32[]{:T(128)} %constant.83.clone.1..sunk) | dynamic-update-slice | bytes 1048580 | tf_op jit(solution)/shard_map/while/body/jit(dynamic_update_index_in_dim)/dynamic_update_slice | solution.py:191
  406.3 11.1 %dynamic_update_slice.29 = f32[4,512,1,256]{1,0,3,2:T(4,128)} dynamic-update-slice(f32[4,512,1,256]{1,0,3,2:T(4,128)} %get-tuple-element.386, f32[1,512,1,256]{1,0,3,2:T(1,128)S(1)} %copy.92, s32[]{:T(128)} %get-tuple-element.385, s32[]{:T(128)} %constant.83.clone.1..sunk, s32[]{:T(128)} %constant.83.clone.1..sunk, s32[]{:T(128)} %constant.83.clone.1..sunk) | dynamic-update-slice | bytes 1048580 | tf_op jit(solution)/shard_map/while/body/jit(dynamic_update_index_in_dim)/dynamic_update_slice | solution.py:191
  425.0 11.0 %dynamic_update_slice.30 = f32[4,512,1,256]{1,0,3,2:T(4,128)} dynamic-update-slice(f32[4,512,1,256]{1,0,3,2:T(4,128)} %get-tuple-element.387, f32[1,512,1,256]{1,0,3,2:T(1,128)S(1)} %copy.93, s32[]{:T(128)} %get-tuple-element.385, s32[]{:T(128)} %constant.83.clone.1..sunk, s32[]{:T(128)} %constant.83.clone.1..sunk, s32[]{:T(128)} %constant.83.clone.1..sunk) | dynamic-update-slice | bytes 1048580 | tf_op jit(solution)/shard_map/while/body/jit(dynamic_update_index_in_dim)/dynamic_update_slice | solution.py:191
  437.8 11.1 %dynamic_update_slice.29 = f32[4,512,1,256]{1,0,3,2:T(4,128)} dynamic-update-slice(f32[4,512,1,256]{1,0,3,2:T(4,128)} %get-tuple-element.386, f32[1,512,1,256]{1,0,3,2:T(1,128)S(1)} %copy.92, s32[]{:T(128)} %get-tuple-element.385, s32[]{:T(128)} %constant.83.clone.1..sunk, s32[]{:T(128)} %constant.83.clone.1..sunk, s32[]{:T(128)} %constant.83.clone.1..sunk) | dynamic-update-slice | bytes 1048580 | tf_op jit(solution)/shard_map/while/body/jit(dynamic_update_index_in_dim)/dynamic_update_slice | solution.py:191
  456.4 11.0 %dynamic_update_slice.30 = f32[4,512,1,256]{1,0,3,2:T(4,128)} dynamic-update-slice(f32[4,512,1,256]{1,0,3,2:T(4,128)} %get-tuple-element.387, f32[1,512,1,256]{1,0,3,2:T(1,128)S(1)} %copy.93, s32[]{:T(128)} %get-tuple-element.385, s32[]{:T(128)} %constant.83.clone.1..sunk, s32[]{:T(128)} %constant.83.clone.1..sunk, s32[]{:T(128)} %constant.83.clone.1..sunk) | dynamic-update-slice | bytes 1048580 | tf_op jit(solution)/shard_map/while/body/jit(dynamic_update_index_in_dim)/dynamic_update_slice | solution.py:191
  469.2 11.1 %dynamic_update_slice.29 = f32[4,512,1,256]{1,0,3,2:T(4,128)} dynamic-update-slice(f32[4,512,1,256]{1,0,3,2:T(4,128)} %get-tuple-element.386, f32[1,512,1,256]{1,0,3,2:T(1,128)S(1)} %copy.92, s32[]{:T(128)} %get-tuple-element.385, s32[]{:T(128)} %constant.83.clone.1..sunk, s32[]{:T(128)} %constant.83.clone.1..sunk, s32[]{:T(128)} %constant.83.clone.1..sunk) | dynamic-update-slice | bytes 1048580 | tf_op jit(solution)/shard_map/while/body/jit(dynamic_update_index_in_dim)/dynamic_update_slice | solution.py:191
  481.5 2.7 reshape.588
  484.2 3.7 reshape.591
  487.9 7.3 fusion.104
  502.2 2.5 add_convert_fusion
  506.5 4.3 fusion.124
  510.8 2.6 fusion.125
  517.0 4.1 fusion.123
  522.9 40.3 %all-reduce.4 = (f32[256]{0:T(256)}, f32[256]{0:T(256)}) all-reduce(f32[256]{0:T(256)S(1)} %get-tuple-element.156, f32[256]{0:T(256)S(1)} %get-tuple-element.154), channel_id=1, replica_groups=mesh['dp'=8,'tensor'=4] {'dp','tensor'}, use_global_device_ids=true, to_apply=%region_33.34 | all-reduce | flops 512 | bytes 4096 | tf_op jit(solution)/shard_map/psum | solution.py:314
  563.1 3.0 all-reduce.21.cloned.1.call-done
  566.2 4.0 fusion.56
  570.2 37.7 %all-reduce.6 = (f32[640]{0:T(1024)}, f32[640]{0:T(1024)}, f32[640]{0:T(1024)}, f32[640]{0:T(1024)}) all-reduce(f32[640]{0:T(1024)S(1)} %get-tuple-element.152, f32[640]{0:T(1024)S(1)} %get-tuple-element.146, f32[640]{0:T(1024)S(1)} %get-tuple-element.148, f32[640]{0:T(1024)S(1)} %get-tuple-element.150), channel_id=1, replica_groups=mesh['dp'=8,'tensor'=4] {'dp'}, use_global_device_ids=true, to_apply=%region_31.32 | all-reduce | flops 2560 | bytes 20480 | tf_op jit(solution)/shard_map/psum | solution.py:327
  607.9 5.5 fusion.60
  613.4 90.6 %all-reduce.23.cloned.1.call-done = (f32[640,256]{1,0:T(8,128)}, f32[640,256]{1,0:T(8,128)}) async-done(((f32[640,256]{1,0:T(8,128)}, f32[640,256]{1,0:T(8,128)}), (f32[640,256]{1,0:T(8,128)}, f32[640,256]{1,0:T(8,128)})) %all-reduce.23.cloned.1.call-update) | async-done | bytes 1310736 | tf_op jit(solution)/shard_map/psum | solution.py:314
  704.0 189.8 %all-reduce.25.cloned.1.call-done = (f32[640,256]{1,0:T(8,128)}, f32[256,640]{1,0:T(8,128)}, f32[640,512]{1,0:T(8,128)}, f32[640,512]{1,0:T(8,128)}, f32[512,640]{1,0:T(8,128)}) async-done(((f32[640,256]{1,0:T(8,128)}, f32[256,640]{1,0:T(8,128)}, f32[640,512]{1,0:T(8,128)}, f32[640,512]{1,0:T(8,128)}, f32[512,640]{1,0:T(8,128)}), (f32[640,256]{1,0:T(8,128)}, f32[256,640]{1,0:T(8,128)}, ...) | async-done | bytes 5242896 | tf_op jit(solution)/shard_map/psum | solution.py:327
  (296 shorter events, 112.7 us)
Async XLA Ops:
  7.2 188.3 %copy-start = (bf16[512,640]{1,0:T(8,128)(2,1)S(1)}, bf16[512,640]{1,0:T(8,128)(2,1)}, u32[]{:S(2)}) copy-start(bf16[512,640]{1,0:T(8,128)(2,1)} %param.28) | copy-start | bytes 1966084
  7.2 2.6 copy-start.4
  7.2 2.6 copy-start.62
  7.2 173.1 %all-reduce.15.cloned.1.call-start = ((), (), s32[]{:S(2)}) async-start(), calls=%async_computation | async-start | bytes 10485760 | tf_op jit(solution)/shard_map/psum | solution.py:263
  7.3 14.0 %copy-start.66 = (f32[128]{0:T(128)}, f32[128]{0:T(128)S(1)}, u32[]{:S(2)}) copy-start(f32[128]{0:T(128)S(1)} %multiply_power_fusion) | copy-start | bytes 1540
  10.8 4.7 copy-start.15
  13.2 5.4 copy-start.46
  15.5 5.8 copy-start.54
  15.5 3.0 copy-start.68
  15.5 3.0 copy-start.69
  15.5 3.0 copy-start.60
  15.6 5.7 copy-start.44
  18.6 2.7 copy-start.56
  18.6 2.7 copy-start.58
  18.6 2.7 copy-start.48
  35.6 3.7 copy-start.61
  74.9 184.1 %all-reduce.17.cloned.1.call-start = ((), (), s32[]{:S(2)}) async-start(), calls=%async_computation.1 | async-start | bytes 5242880 | tf_op jit(solution)/shard_map/psum | solution.py:266
  180.3 4.0 copy-start.2
  190.1 4.1 copy-start.70
  198.8 139.5 %all-reduce.19.cloned.1.call-start = ((), (), s32[]{:S(2)}) async-start(), calls=%async_computation.2 | async-start | bytes 5242880 | tf_op jit(solution)/shard_map/psum | solution.py:269
  261.5 4.2 copy-start.12
  261.5 5.7 copy-start.73
  267.2 5.6 copy-start.27
  267.9 4.9 copy-start.37
  278.1 288.0 %all-reduce.21.cloned.1.call-start = ((), (), s32[]{:S(2)}) async-start(), calls=%async_computation.3 | async-start | bytes 5242880 | tf_op jit(solution)/shard_map/psum | solution.py:272
  338.3 4.4 copy-start.13
  338.3 4.8 copy-start.18
  342.7 8.2 slice-start
  343.1 7.8 slice-start.1
  484.2 3.7 copy-start.49
  484.2 3.7 copy-start.67
  487.9 7.4 copy-start.8
  487.9 7.4 copy-start.47
  487.9 7.4 copy-start.59
  504.8 199.2 %all-reduce.23.cloned.1.call-start = ((), (), s32[]{:S(2)}) async-start(), calls=%async_computation.4 | async-start | bytes 2621440 | tf_op jit(solution)/shard_map/psum | solution.py:314
  506.5 4.3 copy-start.20
  510.8 2.6 copy-start.16
  510.8 2.6 copy-start.24
  516.9 4.1 copy-start.17
  517.0 376.8 %all-reduce.25.cloned.1.call-start = ((), (), s32[]{:S(2)}) async-start(), calls=%async_computation.5 | async-start | bytes 10485760 | tf_op jit(solution)/shard_map/psum | solution.py:327
  517.0 4.1 copy-start.22
  522.8 43.3 %copy-start.5 = (bf16[2048,640]{1,0:T(8,128)(2,1)S(1)}, bf16[2048,640]{1,0:T(8,128)(2,1)}, u32[]{:S(2)}) copy-start(bf16[2048,640]{1,0:T(8,128)(2,1)} %param.21) | copy-start | bytes 7864324
  563.1 44.7 %copy-start.51 = (f32[2048]{0:T(1024)S(1)}, f32[2048]{0:T(1024)}, u32[]{:S(2)}) copy-start(f32[2048]{0:T(1024)} %copy-done.50) | copy-start | bytes 24580
  704.0 193.9 %copy-start.34 = (f32[640,256]{1,0:T(8,128)S(1)}, f32[640,256]{1,0:T(8,128)}, u32[]{:S(2)}) copy-start(f32[640,256]{1,0:T(8,128)} %get-tuple-element.413) | copy-start | bytes 1966084
  893.8 4.9 copy-start.35
  893.8 5.8 copy-start.33
  897.9 2.7 copy-start.32
  899.6 3.2 copy-start.1
  (34 other events, 55.9 us)
Sparse Core Ops, SparseCore 0:
  75.0 105.2 all-reduce.14
  198.9 60.0 all-reduce.16
  278.3 59.9 all-reduce.18
  504.9 61.2 all-reduce.20
  572.2 131.7 all-reduce.22
  709.3 184.4 all-reduce.24
where the time goes:
time: 920 us; the launch traced here: 910 us
  waiting for transfers between devices  502 us (55%)
  local copies, waits for them, and re-layouts  153 us (17%)
  matrix products  95.9 us (10%)
  blocking collectives  77.9 us (8%)
  other arithmetic  63.7 us (7%)
  between operations  15.2 us (2%)
    psum x1, waiting for transfers between devices, on_device(): lax.psum((grad_query_weight, grad_output_weight, grad_gate_weight, grad_u...  190 us
    psum x1, waiting for transfers between devices, attention_reduce(): return lax.psum(values, 'tensor')  105 us
    dynamic_update_slice x16, local copies, waits for them, and re-layouts, run_layer(): lax.map(attend_back, (query_packs, key_packs, value_packs, segment_packs,...  92.6 us
    psum x1, waiting for transfers between devices, on_device(): lax.psum((grad_key_weight, grad_value_weight, grad_query_norm, grad_key_n...  90.6 us
    psum x1, waiting for transfers between devices, feed_reduce(): return lax.psum(values.astype(jnp.bfloat16), 'tensor').astype(jnp.float32)  59.6 us
    psum x1, waiting for transfers between devices, feed_back_reduce(): return lax.psum(values.astype(jnp.bfloat16), 'tensor').astype(jnp.float32)  54.6 us
    psum x1, blocking collectives, on_device(): lax.psum((grad_key_weight, grad_value_weight, grad_query_norm, grad_key_n...  40.3 us
    psum x1, blocking collectives, on_device(): lax.psum((grad_query_weight, grad_output_weight, grad_gate_weight, grad_u...  37.7 us
  transfers between devices with their start and end apart: 6, of which 6 were waited for; matrix products, arithmetic and copies ran while one was open for 3% of the time, Pallas kernels for 0%

commit v1 on v0

--- a/solution.py
+++ b/solution.py
@@ -312,7 +312,8 @@
         feed_hook,
     )
     grad_key_weight, grad_value_weight, grad_query_norm, grad_key_norm = lax.psum(
-        (grad_key_weight, grad_value_weight, grad_query_norm, grad_key_norm), ("dp", "tensor")
+        lax.psum((grad_key_weight, grad_value_weight, grad_query_norm, grad_key_norm), "tensor"),
+        "dp",
     )
     (
         grad_query_weight,

time: 920 us -> 865 us (0.940)
  blocking collectives: 77.9 us -> 45.7 us
  waiting for transfers between devices: 502 us -> 478 us
    psum x1, waiting for transfers between devices: 90.6 us -> 20.4 us  [on_device(): lax.psum((grad_key_weight, grad_value_weight, grad_query_norm, grad_key_n...]
    psum x1, waiting for transfers between devices: 3.04 us -> 56 us  [attention_back_reduce(): return lax.psum(values.astype(jnp.bfloat16), 'tensor').astype(jnp.float32)]
    psum x1, blocking collectives: 40.3 us -> 6.19 us  [on_device(): lax.psum((grad_key_weight, grad_value_weight, grad_query_norm, grad_key_n...]
    unnamed x159 -> x157, local copies, waits for them, and re-layouts: 20.7 us -> 19.8 us
  transfers between devices with their start and end apart: 6 -> 6, of which waited for: 6 -> 6; matrix products, arithmetic and copies ran while one was open for 3% -> 4% of each run, Pallas kernels for 0% -> 0%
where the time goes in v1:
time: 865 us; the launch traced here: 855 us
  waiting for transfers between devices  478 us (55%)
  local copies, waits for them, and re-layouts  152 us (18%)
  matrix products  98.7 us (11%)
  other arithmetic  63.9 us (7%)
  blocking collectives  45.7 us (5%)
  between operations  15.2 us (2%)
    psum x1, waiting for transfers between devices, on_device(): lax.psum((grad_query_weight, grad_output_weight, grad_gate_weight, grad_u...  182 us
    psum x1, waiting for transfers between devices, attention_reduce(): return lax.psum(values, 'tensor')  105 us
    dynamic_update_slice x16, local copies, waits for them, and re-layouts, run_layer(): lax.map(attend_back, (query_packs, key_packs, value_packs, segment_packs,...  92.5 us
    psum x1, waiting for transfers between devices, feed_reduce(): return lax.psum(values.astype(jnp.bfloat16), 'tensor').astype(jnp.float32)  59.6 us
    psum x1, waiting for transfers between devices, attention_back_reduce(): return lax.psum(values.astype(jnp.bfloat16), 'tensor').astype(jnp.float32)  56 us
    psum x1, waiting for transfers between devices, feed_back_reduce(): return lax.psum(values.astype(jnp.bfloat16), 'tensor').astype(jnp.float32)  54.6 us
    psum x1, blocking collectives, on_device(): lax.psum((grad_query_weight, grad_output_weight, grad_gate_weight, grad_u...  39.5 us
    reduce_sum x6, other arithmetic, normed(): return values * inverse * (1.0 + norm_gain)  21.5 us
  transfers between devices with their start and end apart: 6, of which 6 were waited for; matrix products, arithmetic and copies ran while one was open for 4% of the time, Pallas kernels for 0%

profile of v1, /device:TPU:0, one launch (start us, length us, event | category | flops | bytes accessed | tf_op | source)
XLA Modules:
  0.0 854.7 jit_solution(2162961058803706571)
XLA Ops:
  7.3 2.5 fusion.63
  10.8 2.4 multiply_reduce_fusion.6
  13.2 2.3 multiply_reduce_fusion.5
  15.6 3.0 copy.42
  18.6 2.6 multiply_bitcast_fusion
  21.4 5.7 fusion.99
  31.1 2.3 pad_maximum_fusion
  33.4 2.3 copy.56
  35.6 3.7 convolution_convert_fusion.4
  40.0 2.3 pad_maximum_fusion.1
  43.3 26.8 %while.26 = (s32[]{:T(128)}, bf16[4,512,1,256]{3,1,0,2:T(8,128)(2,1)}, f32[4,1,512,1]{2,3,1,0:T(1,128)}, bf16[4,512,256]{2,1,0:T(8,128)(2,1)}, s32[4,512]{1,0:T(...) while((s32[]{:T(128)}, bf16[4,512,1,256]{3,1,0,2:T(8,128)(2,1)}, ...), condition=%wide.region_6.7_spmd, body=%wide.region_3.6_spmd.sunk | while | flops 271187456 | bytes 5272153 | solution.py:134
  70.2 4.6 fusion.115
  75.5 104.7 %all-reduce.15.cloned.1.call-done = f32[2048,640]{1,0:T(8,128)} async-done(((f32[2048,640]{1,0:T(8,128)}), f32[2048,640]{1,0:T(8,128)}) %all-reduce.15.cloned.1.call-update) | async-done | bytes 5242896 | tf_op jit(solution)/shard_map/psum | solution.py:263
  180.2 3.0 multiply_reduce_fusion.4
  190.0 4.1 multiply_convert_fusion.3
  195.4 3.3 convolution_convert_fusion.2
  199.4 59.6 %all-reduce.17.cloned.1.call-done = bf16[2048,640]{1,0:T(8,128)(2,1)} async-done(((bf16[2048,640]{1,0:T(8,128)(2,1)}), bf16[2048,640]{1,0:T(8,128)(2,1)}) %all-reduce.17.cloned.1.call-update) | async-done | bytes 2621456 | tf_op jit(solution)/shard_map/psum | solution.py:266
  258.9 2.5 fusion.61
  261.5 4.2 fusion.57
  267.8 4.9 multiply_convert_fusion.2
  274.7 3.3 add_convert_fusion.1
  278.3 5.3 fusion.126
  283.6 54.6 %all-reduce.19.cloned.1.call-done = bf16[2048,640]{1,0:T(8,128)(2,1)} async-done(((bf16[2048,640]{1,0:T(8,128)(2,1)}), bf16[2048,640]{1,0:T(8,128)(2,1)}) %all-reduce.19.cloned.1.call-update) | async-done | bytes 2621456 | tf_op jit(solution)/shard_map/psum | solution.py:269
  338.2 4.4 fusion.55
  343.1 7.7 multiply_reduce_fusion.1
  355.7 125.6 %while.27 = (s32[]{:T(128)}, f32[4,512,1,256]{1,0,3,2:T(4,128)}, f32[4,512,1,256]{1,0,3,2:T(4,128)}, bf16[4,512,1,256]{3,1,0,2:T(8,128)(2,1)}, bf16[4,512,256]{2...) while((s32[]{:T(128)}, f32[4,512,1,256]{1,0,3,2:T(4,128)}, ...), condition=%wide.region_18.19_spmd, body=%wide.region_16.18_spmd.sunk | while | flops 674627072 | bytes 16275081 | solution.py:191
  362.0 11.0 %dynamic_update_slice.30 = f32[4,512,1,256]{1,0,3,2:T(4,128)} dynamic-update-slice(f32[4,512,1,256]{1,0,3,2:T(4,128)} %get-tuple-element.391, f32[1,512,1,256]{1,0,3,2:T(1,128)S(1)} %copy.93, s32[]{:T(128)} %get-tuple-element.389, s32[]{:T(128)} %constant.83.clone.1..sunk, s32[]{:T(128)} %constant.83.clone.1..sunk, s32[]{:T(128)} %constant.83.clone.1..sunk) | dynamic-update-slice | bytes 1048580 | tf_op jit(solution)/shard_map/while/body/jit(dynamic_update_index_in_dim)/dynamic_update_slice | solution.py:191
  374.8 11.0 %dynamic_update_slice.29 = f32[4,512,1,256]{1,0,3,2:T(4,128)} dynamic-update-slice(f32[4,512,1,256]{1,0,3,2:T(4,128)} %get-tuple-element.390, f32[1,512,1,256]{1,0,3,2:T(1,128)S(1)} %copy.92, s32[]{:T(128)} %get-tuple-element.389, s32[]{:T(128)} %constant.83.clone.1..sunk, s32[]{:T(128)} %constant.83.clone.1..sunk, s32[]{:T(128)} %constant.83.clone.1..sunk) | dynamic-update-slice | bytes 1048580 | tf_op jit(solution)/shard_map/while/body/jit(dynamic_update_index_in_dim)/dynamic_update_slice | solution.py:191
  393.4 11.0 %dynamic_update_slice.30 = f32[4,512,1,256]{1,0,3,2:T(4,128)} dynamic-update-slice(f32[4,512,1,256]{1,0,3,2:T(4,128)} %get-tuple-element.391, f32[1,512,1,256]{1,0,3,2:T(1,128)S(1)} %copy.93, s32[]{:T(128)} %get-tuple-element.389, s32[]{:T(128)} %constant.83.clone.1..sunk, s32[]{:T(128)} %constant.83.clone.1..sunk, s32[]{:T(128)} %constant.83.clone.1..sunk) | dynamic-update-slice | bytes 1048580 | tf_op jit(solution)/shard_map/while/body/jit(dynamic_update_index_in_dim)/dynamic_update_slice | solution.py:191
  406.2 11.0 %dynamic_update_slice.29 = f32[4,512,1,256]{1,0,3,2:T(4,128)} dynamic-update-slice(f32[4,512,1,256]{1,0,3,2:T(4,128)} %get-tuple-element.390, f32[1,512,1,256]{1,0,3,2:T(1,128)S(1)} %copy.92, s32[]{:T(128)} %get-tuple-element.389, s32[]{:T(128)} %constant.83.clone.1..sunk, s32[]{:T(128)} %constant.83.clone.1..sunk, s32[]{:T(128)} %constant.83.clone.1..sunk) | dynamic-update-slice | bytes 1048580 | tf_op jit(solution)/shard_map/while/body/jit(dynamic_update_index_in_dim)/dynamic_update_slice | solution.py:191
  424.7 11.0 %dynamic_update_slice.30 = f32[4,512,1,256]{1,0,3,2:T(4,128)} dynamic-update-slice(f32[4,512,1,256]{1,0,3,2:T(4,128)} %get-tuple-element.391, f32[1,512,1,256]{1,0,3,2:T(1,128)S(1)} %copy.93, s32[]{:T(128)} %get-tuple-element.389, s32[]{:T(128)} %constant.83.clone.1..sunk, s32[]{:T(128)} %constant.83.clone.1..sunk, s32[]{:T(128)} %constant.83.clone.1..sunk) | dynamic-update-slice | bytes 1048580 | tf_op jit(solution)/shard_map/while/body/jit(dynamic_update_index_in_dim)/dynamic_update_slice | solution.py:191
  437.6 11.0 %dynamic_update_slice.29 = f32[4,512,1,256]{1,0,3,2:T(4,128)} dynamic-update-slice(f32[4,512,1,256]{1,0,3,2:T(4,128)} %get-tuple-element.390, f32[1,512,1,256]{1,0,3,2:T(1,128)S(1)} %copy.92, s32[]{:T(128)} %get-tuple-element.389, s32[]{:T(128)} %constant.83.clone.1..sunk, s32[]{:T(128)} %constant.83.clone.1..sunk, s32[]{:T(128)} %constant.83.clone.1..sunk) | dynamic-update-slice | bytes 1048580 | tf_op jit(solution)/shard_map/while/body/jit(dynamic_update_index_in_dim)/dynamic_update_slice | solution.py:191
  456.2 11.0 %dynamic_update_slice.30 = f32[4,512,1,256]{1,0,3,2:T(4,128)} dynamic-update-slice(f32[4,512,1,256]{1,0,3,2:T(4,128)} %get-tuple-element.391, f32[1,512,1,256]{1,0,3,2:T(1,128)S(1)} %copy.93, s32[]{:T(128)} %get-tuple-element.389, s32[]{:T(128)} %constant.83.clone.1..sunk, s32[]{:T(128)} %constant.83.clone.1..sunk, s32[]{:T(128)} %constant.83.clone.1..sunk) | dynamic-update-slice | bytes 1048580 | tf_op jit(solution)/shard_map/while/body/jit(dynamic_update_index_in_dim)/dynamic_update_slice | solution.py:191
  469.0 11.0 %dynamic_update_slice.29 = f32[4,512,1,256]{1,0,3,2:T(4,128)} dynamic-update-slice(f32[4,512,1,256]{1,0,3,2:T(4,128)} %get-tuple-element.390, f32[1,512,1,256]{1,0,3,2:T(1,128)S(1)} %copy.92, s32[]{:T(128)} %get-tuple-element.389, s32[]{:T(128)} %constant.83.clone.1..sunk, s32[]{:T(128)} %constant.83.clone.1..sunk, s32[]{:T(128)} %constant.83.clone.1..sunk) | dynamic-update-slice | bytes 1048580 | tf_op jit(solution)/shard_map/while/body/jit(dynamic_update_index_in_dim)/dynamic_update_slice | solution.py:191
  481.3 2.7 reshape.588
  484.0 3.7 reshape.591
  487.7 7.3 fusion.104
  496.7 3.4 fusion.119
  506.6 5.2 add_convert_fusion
  513.6 4.3 fusion.124
  517.9 2.6 fusion.125
  524.5 20.4 %all-reduce.25.cloned.1.call-done = (f32[640,256]{1,0:T(8,128)}, f32[640,256]{1,0:T(8,128)}) async-done(((f32[640,256]{1,0:T(8,128)}, f32[640,256]{1,0:T(8,128)}), (f32[640,256]{1,0:T(8,128)}, f32[640,256]{1,0:T(8,128)})) %all-reduce.25.cloned.1.call-update) | async-done | bytes 1310736 | tf_op jit(solution)/shard_map/psum | solution.py:315
  544.9 6.2 all-reduce.6
  551.1 56.0 %all-reduce.21.cloned.1.call-done = bf16[2048,640]{1,0:T(8,128)(2,1)} async-done(((bf16[2048,640]{1,0:T(8,128)(2,1)}), bf16[2048,640]{1,0:T(8,128)(2,1)}) %all-reduce.21.cloned.1.call-update) | async-done | bytes 2621456 | tf_op jit(solution)/shard_map/psum | solution.py:272
  607.1 4.0 fusion.56
  611.1 39.5 %all-reduce.4 = (f32[640]{0:T(1024)}, f32[256]{0:T(256)}, f32[256]{0:T(256)}, f32[640]{0:T(1024)}, f32[640]{0:T(1024)}, /*index=5*/f32[640]{0:T(1024)}) all-reduce(f32[640]{0:T(1024)S(1)} %get-tuple-element.152, f32[256]{0:T(256)S(1)} %get-tuple-element.205, ...), channel_id=1, replica_groups=mesh['dp'=8,'tensor'=4] {'dp'}, use_global_device_ids=true, to_apply=%region_33.34 | all-reduce | flops 3072 | bytes 24576 | tf_op jit(solution)/shard_map/psum | solution.py:328
  650.6 5.7 fusion.60
  656.3 182.4 %all-reduce.23.cloned.1.call-done = (f32[640,256]{1,0:T(8,128)}, f32[640,256]{1,0:T(8,128)}, f32[640,256]{1,0:T(8,128)}, f32[256,640]{1,0:T(8,128)}, f32[640,512...) async-done(((f32[640,256]{1,0:T(8,128)}, f32[640,256]{1,0:T(8,128)}, f32[640,256]{1,0:T(8,128)}, f32[256,640]{1,0:T(8,128)}, f32[640,512]{1,0:T(8,128)}, ...) | async-done | bytes 6553616 | tf_op jit(solution)/shard_map/psum | solution.py:328
  (294 shorter events, 112.4 us)
Async XLA Ops:
  7.2 188.2 %copy-start = (bf16[512,640]{1,0:T(8,128)(2,1)S(1)}, bf16[512,640]{1,0:T(8,128)(2,1)}, u32[]{:S(2)}) copy-start(bf16[512,640]{1,0:T(8,128)(2,1)} %param.28) | copy-start | bytes 1966084
  7.2 2.6 copy-start.4
  7.2 2.6 copy-start.61
  7.2 173.0 %all-reduce.15.cloned.1.call-start = ((), (), s32[]{:S(2)}) async-start(), calls=%async_computation | async-start | bytes 10485760 | tf_op jit(solution)/shard_map/psum | solution.py:263
  7.3 14.1 %copy-start.65 = (f32[128]{0:T(128)}, f32[128]{0:T(128)S(1)}, u32[]{:S(2)}) copy-start(f32[128]{0:T(128)S(1)} %multiply_power_fusion) | copy-start | bytes 1540
  10.8 4.7 copy-start.15
  13.2 5.4 copy-start.45
  15.5 5.8 copy-start.53
  15.5 3.0 copy-start.67
  15.5 3.0 copy-start.68
  15.6 3.0 copy-start.59
  15.6 5.7 copy-start.43
  18.6 2.7 copy-start.55
  18.6 2.7 copy-start.57
  18.6 2.7 copy-start.47
  35.6 3.7 copy-start.60
  74.8 184.1 %all-reduce.17.cloned.1.call-start = ((), (), s32[]{:S(2)}) async-start(), calls=%async_computation.1 | async-start | bytes 5242880 | tf_op jit(solution)/shard_map/psum | solution.py:266
  180.2 4.0 copy-start.2
  190.0 4.1 copy-start.69
  198.7 139.5 %all-reduce.19.cloned.1.call-start = ((), (), s32[]{:S(2)}) async-start(), calls=%async_computation.2 | async-start | bytes 5242880 | tf_op jit(solution)/shard_map/psum | solution.py:269
  258.9 2.5 copy-start.7
  261.5 4.2 copy-start.12
  261.5 5.7 copy-start.72
  267.1 5.6 copy-start.25
  267.8 4.9 copy-start.36
  278.1 266.8 %all-reduce.25.cloned.1.call-start = ((), (), s32[]{:S(2)}) async-start(), calls=%async_computation.5 | async-start | bytes 2621440 | tf_op jit(solution)/shard_map/psum | solution.py:315
  338.2 4.4 copy-start.13
  338.2 4.8 copy-start.18
  342.6 8.2 slice-start
  343.1 7.8 slice-start.1
  484.0 3.7 copy-start.48
  484.0 3.7 copy-start.66
  487.6 7.4 copy-start.8
  487.7 7.4 copy-start.46
  487.7 7.4 copy-start.58
  496.7 3.4 copy-start.16
  505.5 101.5 %all-reduce.21.cloned.1.call-start = ((), (), s32[]{:S(2)}) async-start(), calls=%async_computation.3 | async-start | bytes 5242880 | tf_op jit(solution)/shard_map/psum | solution.py:272
  511.9 326.8 %all-reduce.23.cloned.1.call-start = ((), (), s32[]{:S(2)}) async-start(), calls=%async_computation.4 | async-start | bytes 13107200 | tf_op jit(solution)/shard_map/psum | solution.py:328
  513.6 4.3 copy-start.20
  517.9 2.6 copy-start.21
  517.9 2.6 copy-start.27
  544.9 62.2 %copy-start.5 = (bf16[2048,640]{1,0:T(8,128)(2,1)S(1)}, bf16[2048,640]{1,0:T(8,128)(2,1)}, u32[]{:S(2)}) copy-start(bf16[2048,640]{1,0:T(8,128)(2,1)} %param.21) | copy-start | bytes 7864324
  551.1 99.5 %copy-start.50 = (f32[2048]{0:T(1024)S(1)}, f32[2048]{0:T(1024)}, u32[]{:S(2)}) copy-start(f32[2048]{0:T(1024)} %copy-done.49) | copy-start | bytes 24580
  838.7 4.1 copy-start.34
  838.7 4.9 copy-start.33
  838.7 5.8 copy-start.32
  842.8 2.7 copy-start.31
  844.5 3.2 copy-start.1
  (33 other events, 54.4 us)
Sparse Core Ops, SparseCore 0:
  74.9 105.2 all-reduce.14
  198.8 60.0 all-reduce.16
  278.2 59.9 all-reduce.18
  505.6 39.1 all-reduce.24
  547.1 59.9 all-reduce.20
  613.5 225.1 all-reduce.22
